TPU v7x, 256 devices: a whole 4x4x8 slice. The times are simulated.
256 devices in a mesh: group: 16 (over y, z_lo, core), tensor: 16 (over z_hi, x).
Axes of the slice: x: 4, y: 4, z: 8 (z_hi: 4, z_lo: 2; z = z_hi * 2 + z_lo), core: 2. Of those that a mesh axis runs over, the one named last changes fastest.
Arguments:
- queries: bfloat16 [2048, 8192], P('group', 'tensor'), may hold values from -70 to 70
- keys_new: bfloat16 [2048, 2048], P('group', 'tensor'), may hold values from -6 to 6, as said below
- values_new: bfloat16 [2048, 2048], P('group', 'tensor'), may hold values from -6 to 6, as said below
- cache_keys: bfloat16 [64, 16, 512, 128], P('group', 'tensor'), may hold values from -6 to 6, as said below
- cache_values: bfloat16 [64, 16, 512, 128], P('group', 'tensor'), may hold values from -6 to 6, as said below
- cache_len: int32 [64], P('group'), may hold values from 128 to 512, as said below
- accepted: int32 [64], P('group'), may hold values from 1 to 32, as said below
- entering: bfloat16 [2048, 8192], P('group', 'tensor'), may hold values from -6 to 6
- low_feature: bfloat16 [2048, 8192], P('group', 'tensor'), may hold values from -6 to 6
- mid_feature: bfloat16 [2048, 8192], P('group', 'tensor'), may hold values from -6 to 6
- out_proj: bfloat16 [8192, 8192], P('tensor'), may hold values from -0.0625 to 0.0625
- join_weight: bfloat16 [3, 8192, 4096], P(None, 'tensor', 'group'), may hold values from -0.0390625 to 0.0390625
- teacher: bfloat16 [2048, 4096], P('group'), may hold values from -6 to 6
Outputs:
- high_feature: bfloat16 [2048, 8192], P('group', 'tensor')
- draft_grad: float32 [3, 8192, 4096], P(None, 'tensor', 'group')
Inputs may be any that keep to these rules, and one draw needn't show every extreme that they name: `cache_len`: the first sequence of every group fills all 512 slots. `accepted`: the last sequence accepts all 32 tokens. `cache_keys`: entries t and u of the second dimension are equal where t * 8 // 16 equals u * 8 // 16. `cache_values`: entries t and u of the second dimension are equal where t * 8 // 16 equals u * 8 // 16. `keys_new`: column blocks t and u of 128 columns are equal where t * 8 // 16 equals u * 8 // 16. `values_new`: column blocks t and u of 128 columns are equal where t * 8 // 16 equals u * 8 // 16.
All inputs are finite; a program needn't handle non-finite values.
Results may differ from a plain program's by a relative error of at most 0.0065.
Values may be sent and summed in bfloat16 or wider, within the bound.
A program may use at most 128 MiB of HBM per device.

v0:
```python
import jax
import jax.numpy as jnp
from jax import lax
from jax.sharding import PartitionSpec as P


def attend(query, key_new, value_new, cache_keys, cache_values, cache_len):
    scale = query.shape[-1] ** (-0.5)
    s_cache = (
        jnp.einsum("spkhe,skle->skhpl", query, cache_keys, preferred_element_type=jnp.float32)
        * scale
    )
    s_new = (
        jnp.einsum("spkhe,sqke->skhpq", query, key_new, preferred_element_type=jnp.float32) * scale
    )
    slots = jnp.arange(cache_keys.shape[2], dtype=jnp.int32)
    filled = slots[None, :] < cache_len[:, None]
    s_cache = jnp.where(filled[:, None, None, None, :], s_cache, -jnp.inf)
    places = jnp.arange(query.shape[1], dtype=jnp.int32)
    causal = places[None, :] <= places[:, None]
    s_new = jnp.where(causal, s_new, -jnp.inf)
    top = jnp.maximum(jnp.max(s_cache, axis=-1), jnp.max(s_new, axis=-1))
    p_cache = jnp.exp(s_cache - top[..., None])
    p_new = jnp.exp(s_new - top[..., None])
    total = jnp.sum(p_cache, axis=-1) + jnp.sum(p_new, axis=-1)
    mixed = jnp.einsum(
        "skhpl,skle->skhpe",
        p_cache.astype(jnp.bfloat16),
        cache_values,
        preferred_element_type=jnp.float32,
    )
    mixed = mixed + jnp.einsum(
        "skhpq,sqke->skhpe",
        p_new.astype(jnp.bfloat16),
        value_new,
        preferred_element_type=jnp.float32,
    )
    result = (mixed / total[..., None]).astype(jnp.bfloat16)
    return result.transpose(0, 3, 1, 2, 4)


def shards(
    queries,
    keys_new,
    values_new,
    cache_keys,
    cache_values,
    cache_len,
    accepted,
    entering,
    low_feature,
    mid_feature,
    out_proj,
    join_weight,
    teacher,
):
    seqs = cache_len.shape[0]
    kv_local = cache_keys.shape[1]
    depth = cache_keys.shape[3]
    rows = keys_new.shape[0]
    places = rows // seqs
    per_kv = queries.shape[1] // (kv_local * depth)
    query_s = queries.reshape(seqs, places, kv_local, per_kv, depth)
    key_s = keys_new.reshape(seqs, places, kv_local, depth)
    value_s = values_new.reshape(seqs, places, kv_local, depth)
    attended = attend(query_s, key_s, value_s, cache_keys, cache_values, cache_len).reshape(
        rows, queries.shape[1]
    )
    partial_value = jnp.dot(attended, out_proj, preferred_element_type=jnp.float32)
    projected = lax.psum_scatter(partial_value, "tensor", scatter_dimension=1, tiled=True)
    high_feature = (entering.astype(jnp.float32) + projected).astype(jnp.bfloat16)
    features = jnp.concatenate([low_feature, mid_feature, high_feature], axis=1)
    local_weight = join_weight.reshape(-1, join_weight.shape[2])
    gathered = lax.all_gather(features, "group", axis=0, tiled=True)
    joined_part = jnp.dot(
        features,
        lax.all_gather(local_weight, "group", axis=1, tiled=True),
        preferred_element_type=jnp.float32,
    )
    place = jnp.arange(rows, dtype=jnp.int32) % places
    live = place < jnp.repeat(accepted, places)
    scale = seqs / jnp.sum(accepted.astype(jnp.float32))
    joined = lax.psum(joined_part, "tensor")
    error = (joined - teacher.astype(jnp.float32)) * scale
    error = jnp.where(live[:, None], error, jnp.zeros_like(error)).astype(jnp.bfloat16)
    error_cols = lax.all_to_all(error, "group", split_axis=1, concat_axis=0, tiled=True)
    draft_grad = lax.dot_general(
        gathered, error_cols, (((0,), (0,)), ((), ())), preferred_element_type=jnp.float32
    )
    return (high_feature, draft_grad.reshape(join_weight.shape))


def solution(mesh):
    return jax.shard_map(
        shards,
        mesh=mesh,
        in_specs=(
            P("group", "tensor"),
            P("group", "tensor"),
            P("group", "tensor"),
            P("group", "tensor", None, None),
            P("group", "tensor", None, None),
            P("group"),
            P("group"),
            P("group", "tensor"),
            P("group", "tensor"),
            P("group", "tensor"),
            P("tensor", None),
            P(None, "tensor", "group"),
            P("group", None),
        ),
        out_specs=(P("group", "tensor"), P(None, "tensor", "group")),
        check_vma=False,
    )
```

profile of v0, /device:TPU:1, one launch (start us, length us, event | category | flops | bytes accessed | tf_op | source)
XLA Modules:
  0.0 407.3 jit_solution(14974270197257214608)
XLA Ops:
  8.1 0.8 iota_compare_fusion.1
  8.9 0.9 reshape.122
  9.8 1.1 fusion.29
  10.9 0.4 fusion.28
  11.3 0.1 fusion.16
  11.4 0.3 fusion.8
  11.7 1.4 fusion.11
  13.1 0.3 fusion.7
  13.4 0.1 copy.29
  13.5 6.6 %fusion.20 = f32[128,8192]{1,0:T(8,128)} fusion(bf16[512,8192]{1,0:T(8,128)(2,1)} %param.23, bf16[16,8,4,128]{3,2,1,0:T(4,128)(2,1)S(1)} %bitcast.77), kind=kOutput, calls=%fused_computation.27 | convolution fusion | flops 1073741824 | bytes 12713984 | tf_op jit(solution)/shard_map/dot_general | solution.py:69
  20.1 0.5 all-gather.5.cloned.1.call-update
  20.7 147.2 %reduce-scatter.2.cloned.1.call-done = f32[128,512]{1,0:T(8,128)} async-done(((f32[128,8192]{1,0:T(8,128)}), f32[128,512]{1,0:T(8,128)}) %reduce-scatter.2.cloned.1.call-update) | async-done | bytes 262160 | tf_op jit(solution)/shard_map/reduce_scatter | solution.py:70
  168.0 1.0 add_convert_fusion
  169.0 7.8 %fusion.27 = f32[128,4096]{1,0:T(8,128)} fusion(bf16[1536,4096]{1,0:T(8,128)(2,1)} %all-gather.5.cloned.1.call-done, bf16[128,512]{1,0:T(8,128)(2,1)S(1)} %add_convert_fusion, bf16[128,512]{1,0:T(8,128)(2,1)S(1)} %copy-done.3, bf16[128,512]{1,0:T(8,128)(2,1)S(1)} %copy-done.4), kind=kOutput, calls=%fused_computation.38 | convolution fusion | flops 1611792384 | bytes 15073280 | tf_op jit(solution)/shard_map/dot_general | solution.py:75
  176.9 0.8 pad_maximum_fusion
  177.8 0.1 reshape.129
  177.9 0.6 convert_reduce_fusion
  179.2 182.9 %all-reduce.2.cloned.1.call-done = f32[128,4096]{1,0:T(8,128)} async-done(((f32[128,4096]{1,0:T(8,128)}), f32[128,4096]{1,0:T(8,128)}) %all-reduce.2.cloned.1.call-update) | async-done | bytes 2097168 | tf_op jit(solution)/shard_map/psum | solution.py:83
  362.2 1.9 select_convert_fusion
  364.1 1.1 copy.52
  365.2 13.1 %all-to-all-start = ((bf16[128,16,256]{2,0,1:T(8,128)(2,1)}), bf16[128,16,256]{2,0,1:T(8,128)(2,1)S(1)}, u32[]{:S(2)}, u32[]{:S(2)}) async-start(bf16[128,16,256]{2,0,1:T(8,128)(2,1)} %bitcast.71), calls=%async_computation.1 | async-start | bytes 2097152 | tf_op jit(solution)/shard_map/all_to_all | solution.py:86
  378.3 8.7 %copy.30 = bf16[1536,2048]{1,0:T(8,128)(2,1)} copy(bf16[1536,2048]{0,1:T(8,128)(2,1)} %bitcast.72) | data formatting | bytes 12582912 | tf_op jit(solution)/shard_map/dot_general | solution.py:87
  387.0 7.1 %all-to-all-done = bf16[128,16,256]{2,0,1:T(8,128)(2,1)S(1)} async-done(((bf16[128,16,256]{2,0,1:T(8,128)(2,1)}), bf16[128,16,256]{2,0,1:T(8,128)(2,1)S(1)}, u32[]{:S(2)}, u32[]{:S(2)}) %all-to-all-start) | async-done | bytes 1048608 | tf_op jit(solution)/shard_map/all_to_all | solution.py:86
  394.1 5.7 %fusion.30 = f32[3,512,256]{2,1,0:T(8,128)} fusion(bf16[3,512,2048]{2,1,0:T(8,128)(2,1)} %bitcast.73, bf16[2048,256,1]{1,0,2:T(8,128)(2,1)S(1)} %bitcast.75), kind=kOutput, calls=%fused_computation.41 | convolution fusion | flops 1610612736 | bytes 8912896 | tf_op jit(solution)/shard_map/dot_general | solution.py:87
  (30 shorter events, 0.4 us)
Async XLA Ops:
  8.0 2.9 copy-start
  8.0 5.1 %copy-start.7 = (bf16[128,128]{1,0:T(8,128)(2,1)S(1)}, bf16[128,128]{1,0:T(8,128)(2,1)}, u32[]{:S(2)}) copy-start(bf16[128,128]{1,0:T(8,128)(2,1)} %param.15) | copy-start | bytes 98308
  8.0 159.9 %reduce-scatter.2.cloned.1.call-start = ((), (), s32[]{:S(2)}) async-start(), calls=%async_computation.2 | async-start | bytes 4456448 | tf_op jit(solution)/shard_map/reduce_scatter | solution.py:70
  20.1 147.9 %copy-start.5 = (bf16[128,512]{1,0:T(8,128)(2,1)S(1)}, bf16[128,512]{1,0:T(8,128)(2,1)}, u32[]{:S(2)}) copy-start(bf16[128,512]{1,0:T(8,128)(2,1)} %param.20) | copy-start | bytes 393220
  20.1 148.9 %copy-start.3 = (bf16[128,512]{1,0:T(8,128)(2,1)S(1)}, bf16[128,512]{1,0:T(8,128)(2,1)}, u32[]{:S(2)}) copy-start(bf16[128,512]{1,0:T(8,128)(2,1)} %param.22) | copy-start | bytes 393220
  20.1 149.0 %copy-start.4 = (bf16[128,512]{1,0:T(8,128)(2,1)S(1)}, bf16[128,512]{1,0:T(8,128)(2,1)}, u32[]{:S(2)}) copy-start(bf16[128,512]{1,0:T(8,128)(2,1)} %param.21) | copy-start | bytes 393220
  20.1 148.9 %all-gather.5.cloned.1.call-start = ((), (), s32[]{:S(2)}) async-start(), calls=%async_computation.4 | async-start | bytes 13369344 | tf_op jit(solution)/shard_map/all_gather | solution.py:77
  20.7 341.5 %all-reduce.2.cloned.1.call-start = ((), (), s32[]{:S(2)}) async-start(), calls=%async_computation.5 | async-start | bytes 4194304 | tf_op jit(solution)/shard_map/psum | solution.py:83
  168.9 8.0 %copy-start.1 = (bf16[128,512]{1,0:T(8,128)(2,1)}, bf16[128,512]{1,0:T(8,128)(2,1)S(1)}, u32[]{:S(2)}) copy-start(bf16[128,512]{1,0:T(8,128)(2,1)S(1)} %add_convert_fusion) | copy-start | bytes 393220
  169.0 8.8 %copy-start.6 = (s32[4]{0:T(128)S(1)}, s32[4]{0:T(128)}, u32[]{:S(2)}) copy-start(s32[4]{0:T(128)} %param.19) | copy-start | bytes 52
  169.0 193.2 %copy-start.2 = (bf16[128,4096]{1,0:T(8,128)(2,1)S(1)}, bf16[128,4096]{1,0:T(8,128)(2,1)}, u32[]{:S(2)}) copy-start(bf16[128,4096]{1,0:T(8,128)(2,1)} %param.25) | copy-start | bytes 3145732
  176.9 201.4 %all-gather.3.cloned.1.call-start = ((), (), s32[]{:S(2)}) async-start(), calls=%async_computation.3 | async-start | bytes 6684672 | tf_op jit(solution)/shard_map/all_gather | solution.py:74
  365.2 28.9 %all-to-all-start = ((bf16[128,16,256]{2,0,1:T(8,128)(2,1)}), bf16[128,16,256]{2,0,1:T(8,128)(2,1)S(1)}, u32[]{:S(2)}, u32[]{:S(2)}) async-start(bf16[128,16,256]{2,0,1:T(8,128)(2,1)} %bitcast.71), calls=%async_computation.1 | async-start | bytes 2097152 | tf_op jit(solution)/shard_map/all_to_all | solution.py:86
Sparse Core Ops, SparseCore 0:
  20.2 147.6 reduce-scatter.1
  177.0 185.1 all-reduce.1
Sparse Core Ops, SparseCore 1:
  22.5 99.3 all-gather.4
  179.3 58.5 all-gather.2
where the time goes:
time: 408 us; the launch traced here: 407 us
  waiting for transfers between devices  338 us (83%)
  matrix products  23.2 us (6%)
  between operations  16.3 us (4%)
  starting transfers between devices  13.2 us (3%)
  local copies, waits for them, and re-layouts  11 us (3%)
  other arithmetic  5.55 us (1%)
    psum x1, waiting for transfers between devices, shards(): joined = lax.psum(joined_part, 'tensor')  183 us
    reduce_scatter x1, waiting for transfers between devices, shards(): lax.psum_scatter(partial_value, 'tensor', scatter_dimension=1, tiled=True)  147 us
    all_to_all x1, starting transfers between devices, shards(): lax.all_to_all(error, 'group', split_axis=1, concat_axis=0, tiled=True)  13.1 us
    dot_general x1, local copies, waits for them, and re-layouts, shards(): lax.dot_general(gathered, error_cols, (((0,), (0,)), ((), ())), preferred...  8.67 us
  transfers between devices with their start and end apart: 5, of which 3 were waited for; matrix products, arithmetic and copies ran while one was open for 3% of the time, Pallas kernels for 0%

commit v1 on v0

--- a/solution.py
+++ b/solution.py
@@ -80,7 +80,7 @@
     place = jnp.arange(rows, dtype=jnp.int32) % places
     live = place < jnp.repeat(accepted, places)
     scale = seqs / jnp.sum(accepted.astype(jnp.float32))
-    joined = lax.psum(joined_part, "tensor")
+    joined = jnp.sum(lax.all_gather(joined_part, "tensor"), axis=0)
     error = (joined - teacher.astype(jnp.float32)) * scale
     error = jnp.where(live[:, None], error, jnp.zeros_like(error)).astype(jnp.bfloat16)
     error_cols = lax.all_to_all(error, "group", split_axis=1, concat_axis=0, tiled=True)

time: 408 us -> 629 us (1.54)
  waiting for transfers between devices: 338 us -> 555 us
  other arithmetic: 5.55 us -> 17.2 us
  starting transfers between devices: 13.2 us -> 5.03 us
    all_gather x0 -> x1, waiting for transfers between devices: none -> 369 us  [shards(): joined = jnp.sum(lax.all_gather(joined_part, 'tensor'), axis=0)]
    psum x1 -> x0, waiting for transfers between devices: 183 us -> none  [shards(): joined = lax.psum(joined_part, 'tensor')]
    all_gather x1, waiting for transfers between devices: 0.02 us -> 37.6 us  [shards(): gathered = lax.all_gather(features, 'group', axis=0, tiled=True)]
    reduce_sum x0 -> x1, other arithmetic: none -> 11.8 us  [shards(): joined = jnp.sum(lax.all_gather(joined_part, 'tensor'), axis=0)]
    all_to_all x1, starting transfers between devices: 13.1 us -> 4.87 us  [shards(): lax.all_to_all(error, 'group', split_axis=1, concat_axis=0, tiled=True)]
    all_to_all x1, waiting for transfers between devices: 7.13 us -> 0.01 us  [shards(): lax.all_to_all(error, 'group', split_axis=1, concat_axis=0, tiled=True)]
  transfers between devices with their start and end apart: 5 -> 5, of which waited for: 3 -> 3; matrix products, arithmetic and copies ran while one was open for 3% -> 4% of each run, Pallas kernels for 0% -> 0%
where the time goes in v1:
time: 629 us; the launch traced here: 628 us
  waiting for transfers between devices  555 us (88%)
  matrix products  24 us (4%)
  other arithmetic  17.2 us (3%)
  between operations  16 us (3%)
  local copies, waits for them, and re-layouts  11.1 us (2%)
    all_gather x1, waiting for transfers between devices, shards(): joined = jnp.sum(lax.all_gather(joined_part, 'tensor'), axis=0)  369 us
    reduce_scatter x1, waiting for transfers between devices, shards(): lax.psum_scatter(partial_value, 'tensor', scatter_dimension=1, tiled=True)  147 us
    all_gather x1, waiting for transfers between devices, shards(): gathered = lax.all_gather(features, 'group', axis=0, tiled=True)  37.6 us
  transfers between devices with their start and end apart: 5, of which 3 were waited for; matrix products, arithmetic and copies ran while one was open for 4% of the time, Pallas kernels for 0%

profile of v1, /device:TPU:1, one launch (start us, length us, event | category | flops | bytes accessed | tf_op | source)
XLA Modules:
  0.0 627.8 jit_solution(4018947574373349039)
XLA Ops:
  8.1 0.8 iota_compare_fusion.1
  8.8 0.9 reshape.122
  9.8 1.1 fusion.29
  10.9 0.4 fusion.28
  11.3 0.1 fusion.16
  11.4 0.3 fusion.8
  11.7 1.4 fusion.11
  13.1 1.0 fusion.7
  14.3 6.6 %fusion.20 = f32[128,8192]{1,0:T(8,128)} fusion(bf16[512,8192]{1,0:T(8,128)(2,1)} %param.23, bf16[16,8,4,128]{3,2,1,0:T(4,128)(2,1)S(1)} %bitcast.79), kind=kOutput, calls=%fused_computation.27 | convolution fusion | flops 1073741824 | bytes 12713984 | tf_op jit(solution)/shard_map/dot_general | solution.py:69
  21.0 0.5 all-gather.7.cloned.1.call-update
  21.6 147.2 %reduce-scatter.2.cloned.1.call-done = f32[128,512]{1,0:T(8,128)} async-done(((f32[128,8192]{1,0:T(8,128)}), f32[128,512]{1,0:T(8,128)}) %reduce-scatter.2.cloned.1.call-update) | async-done | bytes 262160 | tf_op jit(solution)/shard_map/reduce_scatter | solution.py:70
  168.8 1.0 add_convert_fusion
  169.8 7.7 %fusion.27 = f32[128,4096]{1,0:T(8,128)} fusion(bf16[1536,4096]{1,0:T(8,128)(2,1)} %all-gather.7.cloned.1.call-done, bf16[128,512]{1,0:T(8,128)(2,1)S(1)} %add_convert_fusion, bf16[128,512]{1,0:T(8,128)(2,1)S(1)} %copy-done.3, bf16[128,512]{1,0:T(8,128)(2,1)S(1)} %copy-done.4), kind=kOutput, calls=%fused_computation.38 | convolution fusion | flops 1611792384 | bytes 15073280 | tf_op jit(solution)/shard_map/dot_general | solution.py:75
  177.6 0.8 pad_maximum_fusion
  178.5 0.1 reshape.129
  178.6 0.6 convert_reduce_fusion
  179.9 369.1 %all-gather.9.cloned.1.call-done = f32[2048,4096]{1,0:T(8,128)} async-done(((f32[128,4096]{1,0:T(8,128)}), f32[2048,4096]{1,0:T(8,128)}) %all-gather.9.cloned.1.call-update) | async-done | bytes 33554448 | tf_op jit(solution)/shard_map/all_gather | solution.py:83
  549.0 11.8 %reduce_sum.38 = f32[128,4096]{1,0:T(8,128)S(1)} reduce(f32[16,128,4096]{2,1,0:T(8,128)} %bitcast.73, f32[]{:T(128)} %constant.21.clone.1), dimensions={0}, to_apply=%region_5.6 | reduce | flops 7864320 | bytes 35651588 | tf_op jit(solution)/shard_map/reduce_sum | solution.py:83
  560.8 1.8 select_convert_fusion
  562.6 1.1 copy.46
  563.7 4.9 all-to-all-start
  568.6 37.6 %all-gather.5.cloned.1.call-done = bf16[2048,1536]{1,0:T(8,128)(2,1)} async-done(((bf16[128,1536]{1,0:T(8,128)(2,1)}), bf16[2048,1536]{1,0:T(8,128)(2,1)}) %all-gather.5.cloned.1.call-update) | async-done | bytes 6291472 | tf_op jit(solution)/shard_map/all_gather | solution.py:74
  606.2 8.8 %copy.24 = bf16[1536,2048]{1,0:T(8,128)(2,1)} copy(bf16[1536,2048]{0,1:T(8,128)(2,1)} %bitcast.74) | data formatting | bytes 12582912 | tf_op jit(solution)/shard_map/dot_general | solution.py:87
  615.0 5.7 fusion.30
  (29 shorter events, 0.5 us)
Async XLA Ops:
  8.0 2.9 copy-start
  8.0 160.7 %reduce-scatter.2.cloned.1.call-start = ((), (), s32[]{:S(2)}) async-start(), calls=%async_computation.2 | async-start | bytes 4456448 | tf_op jit(solution)/shard_map/reduce_scatter | solution.py:70
  14.2 154.5 %copy-start.5 = (bf16[128,512]{1,0:T(8,128)(2,1)S(1)}, bf16[128,512]{1,0:T(8,128)(2,1)}, u32[]{:S(2)}) copy-start(bf16[128,512]{1,0:T(8,128)(2,1)} %param.20) | copy-start | bytes 393220
  14.2 155.6 %copy-start.3 = (bf16[128,512]{1,0:T(8,128)(2,1)S(1)}, bf16[128,512]{1,0:T(8,128)(2,1)}, u32[]{:S(2)}) copy-start(bf16[128,512]{1,0:T(8,128)(2,1)} %param.22) | copy-start | bytes 393220
  14.2 155.6 %copy-start.4 = (bf16[128,512]{1,0:T(8,128)(2,1)S(1)}, bf16[128,512]{1,0:T(8,128)(2,1)}, u32[]{:S(2)}) copy-start(bf16[128,512]{1,0:T(8,128)(2,1)} %param.21) | copy-start | bytes 393220
  20.9 148.9 %all-gather.7.cloned.1.call-start = ((), (), s32[]{:S(2)}) async-start(), calls=%async_computation.4 | async-start | bytes 13369344 | tf_op jit(solution)/shard_map/all_gather | solution.py:77
  21.5 527.5 %all-gather.9.cloned.1.call-start = ((), (), s32[]{:S(2)}) async-start(), calls=%async_computation.5 | async-start | bytes 35651584 | tf_op jit(solution)/shard_map/all_gather | solution.py:83
  169.7 7.9 %copy-start.2 = (bf16[128,512]{1,0:T(8,128)(2,1)}, bf16[128,512]{1,0:T(8,128)(2,1)S(1)}, u32[]{:S(2)}) copy-start(bf16[128,512]{1,0:T(8,128)(2,1)S(1)} %add_convert_fusion) | copy-start | bytes 393220
  169.8 8.7 %copy-start.6 = (s32[4]{0:T(128)S(1)}, s32[4]{0:T(128)}, u32[]{:S(2)}) copy-start(s32[4]{0:T(128)} %param.19) | copy-start | bytes 52
  177.6 428.6 %all-gather.5.cloned.1.call-start = ((), (), s32[]{:S(2)}) async-start(), calls=%async_computation.3 | async-start | bytes 6684672 | tf_op jit(solution)/shard_map/all_gather | solution.py:74
  563.7 51.2 %all-to-all-start = ((bf16[128,16,256]{2,0,1:T(8,128)(2,1)}), bf16[128,16,256]{2,0,1:T(8,128)(2,1)S(1)}, u32[]{:S(2)}, u32[]{:S(2)}) async-start(bf16[128,16,256]{2,0,1:T(8,128)(2,1)} %bitcast.72), calls=%async_computation.1 | async-start | bytes 2097152 | tf_op jit(solution)/shard_map/all_to_all | solution.py:86
  606.2 14.5 %copy-start.1 = (bf16[4,1,512,128]{3,2,1,0:T(8,128)(2,1)S(1)}, bf16[4,1,512,128]{3,2,1,0:T(8,128)(2,1)}, u32[]{:S(2)}) copy-start(bf16[4,1,512,128]{3,2,1,0:T(8,128)(2,1)} %param.16) | copy-start | bytes 1572868
Sparse Core Ops, SparseCore 0:
  21.0 147.6 reduce-scatter.1
  177.7 371.3 all-gather.8
  551.0 55.0 all-gather.4
Sparse Core Ops, SparseCore 1:
  23.3 99.3 all-gather.6
